TPU v7x, 256 devices: a whole 4x4x8 slice. The times are simulated.
256 devices in a mesh: ctx: 128 (over x, y, z), head: 2 (over core).
Axes of the slice: x: 4, y: 4, z: 8, core: 2. Of those that a mesh axis runs over, the one named last changes fastest.
Arguments:
- queries: bfloat16 [65536, 2048], P('ctx', 'head'), may hold values from -1.5 to 1.5
- key_vectors: bfloat16 [65536, 2048], P('ctx', 'head'), may hold values from -1.5 to 1.5
- values: bfloat16 [65536, 2048], P('ctx', 'head'), may hold values from -4 to 4
- features: bfloat16 [16, 128, 256], P('head'), may hold values from -4 to 4
- norm_gain: bfloat16 [2048], P('head'), may hold values from 0.099609375 to 1.8984375
- out_weight: bfloat16 [2048, 2048], P('head'), may hold values from -0.125 to 0.125
Outputs:
- projected: bfloat16 [65536, 2048], P(('ctx', 'head'))
All inputs are finite; a program needn't handle non-finite values.
Results may differ from a plain program's by a relative error of at most 0.0059.
Values may be sent and summed in bfloat16 or wider, within the bound.
A program may use at most 320 MiB of HBM per device.

v0:
```python
import jax
import jax.numpy as jnp
from jax import lax
from jax.sharding import PartitionSpec as P

BLK = 256


epsilon = 1e-05


def carried_in(part, axis, combine, identity):
    place = lax.axis_index(axis)
    gathered = lax.all_gather(part, axis)
    state = jnp.zeros_like(part) + jnp.asarray(identity, part.dtype)

    def one(hop, state):
        return combine(state, lax.dynamic_index_in_dim(gathered, hop, 0, False))

    return lax.fori_loop(0, place, one, state)


def positive(vectors, matrix):
    head_size = matrix.shape[1]
    feature_count = matrix.shape[2]
    feature_scale = head_size ** (-0.25)
    linear_part = (
        jnp.einsum("rhd,hdm->rhm", vectors, matrix, preferred_element_type=jnp.float32)
        * feature_scale
    )
    widened = vectors.astype(jnp.float32)
    squares = jnp.sum(widened * widened, axis=-1, keepdims=True) * (feature_scale * feature_scale)
    return (jnp.exp(linear_part - 0.5 * squares) * feature_count ** (-0.5)).astype(jnp.bfloat16)


def combine_state_list(earlier_part, later_part):
    return earlier_part + later_part


def local(queries, key_vectors, values, features, norm_gain, out_weight):
    heads_here, head_size, feature_count = features.shape
    rows_dev = queries.shape[0]
    blocks = rows_dev // BLK
    query_feature_map = positive(
        queries.reshape(rows_dev, heads_here, head_size), features
    ).reshape(blocks, BLK, heads_here, feature_count)
    key_feature_map = positive(
        key_vectors.reshape(rows_dev, heads_here, head_size), features
    ).reshape(blocks, BLK, heads_here, feature_count)
    value_blocks = values.reshape(blocks, BLK, heads_here, head_size)
    block_states = jnp.einsum(
        "bjhm,bjhd->bhmd", key_feature_map, value_blocks, preferred_element_type=jnp.float32
    )
    device_sum = jnp.sum(block_states, axis=0)
    earlier_sum = carried_in(device_sum, "ctx", combine_state_list, jnp.zeros_like(device_sum))
    causal_mask = jnp.arange(BLK)[:, None] >= jnp.arange(BLK)[None, :]
    gain_heads = norm_gain.astype(jnp.float32).reshape(heads_here, head_size)

    def advance(cumulative_state, pieces):
        query_block, key_block, value_tile_rows, block_kv_state = pieces
        scores = jnp.einsum(
            "ihm,jhm->hij", query_block, key_block, preferred_element_type=jnp.float32
        )
        weights = jnp.where(causal_mask[None], scores, jnp.float32(0.0)).astype(jnp.bfloat16)
        local_term = jnp.einsum(
            "hij,jhd->ihd", weights, value_tile_rows, preferred_element_type=jnp.float32
        )
        preceding_block_term = jnp.einsum(
            "gnp,npf->gnf",
            query_block,
            cumulative_state.astype(jnp.bfloat16),
            preferred_element_type=jnp.float32,
        )
        numerator = preceding_block_term + local_term
        normed = (
            numerator
            * lax.rsqrt(jnp.mean(numerator * numerator, axis=-1, keepdims=True) + epsilon)
            * gain_heads
        )
        attended_block = normed.reshape(BLK, heads_here * head_size).astype(jnp.bfloat16)
        return (cumulative_state + block_kv_state, attended_block)

    _, attended = lax.scan(
        advance, earlier_sum, (query_feature_map, key_feature_map, value_blocks, block_states)
    )
    attended = attended.reshape(rows_dev, heads_here * head_size)
    projected = lax.psum_scatter(
        jnp.dot(attended, out_weight, preferred_element_type=jnp.float32),
        "head",
        scatter_dimension=0,
        tiled=True,
    )
    return projected.astype(jnp.bfloat16)


def solution(mesh):
    return jax.shard_map(
        local,
        mesh=mesh,
        in_specs=(
            P("ctx", "head"),
            P("ctx", "head"),
            P("ctx", "head"),
            P("head", None, None),
            P("head"),
            P("head", None),
        ),
        out_specs=P(("ctx", "head"), None),
        check_vma=False,
    )
```

profile of v0, /device:TPU:1, one launch (start us, length us, event | category | flops | bytes accessed | tf_op | source)
XLA Modules:
  0.0 880.0 jit_solution(11827098249829786017)
XLA Ops:
  6.5 1.5 copy.65
  8.8 2.4 fusion.28
  11.2 2.1 reshape.49
  13.3 4.7 copy.55
  17.9 2.2 copy.66
  20.2 3.2 fusion.39
  23.5 1.6 copy.67
  25.8 2.5 fusion.25
  28.2 2.5 reshape.52
  30.8 3.7 copy.53
  34.6 599.3 %all-gather.3.cloned.1.call-done = f32[1024,256,128]{2,1,0:T(8,128)} async-done(((f32[8,256,128]{2,1,0:T(8,128)}), f32[1024,256,128]{2,1,0:T(8,128)}) %all-gather.3.cloned.1.call-update) | async-done | bytes 134217744 | tf_op jit(solution)/shard_map/all_gather | solution.py:14
  634.3 26.1 %while.24 = (s32[]{:T(128)}, f32[8,256,128]{1,2,0:T(8,128)S(1)}, bf16[2,256,1024]{2,1,0:T(8,128)(2,1)}, f32[2,8,256,128]{3,2,1,0:T(8,128)}, bf16[2,256,8,256]{3,...) while((s32[]{:T(128)}, f32[8,256,128]{1,2,0:T(8,128)S(1)}, ...), condition=%wide.region_7.8_spmd.clone, body=%wide.region_5.7_spmd.clone.sunk | while | flops 540084224 | bytes 25335936 | solution.py:83
  634.3 1.8 convolution_bitcast_fusion.2
  637.3 3.4 multiply_reduce_fusion.4
  640.8 1.4 multiply_convert_fusion.2
  643.2 2.3 constant_dynamic-slice_fusion.4
  645.5 1.6 copy.83
  647.4 1.8 convolution_bitcast_fusion.2
  650.3 3.4 multiply_reduce_fusion.4
  656.3 2.3 constant_dynamic-slice_fusion.4
  658.6 1.6 copy.83
  660.4 6.8 fusion.40
  667.2 203.3 %reduce-scatter.2.cloned.1.call-done = f32[256,2048]{1,0:T(8,128)} async-done(((f32[512,2048]{1,0:T(8,128)}), f32[256,2048]{1,0:T(8,128)}) %reduce-scatter.2.cloned.1.call-update) | async-done | bytes 2097168 | tf_op jit(solution)/shard_map/reduce_scatter | solution.py:87
  870.5 2.7 convert_element_type.42
  (44 shorter events, 8.3 us)
Async XLA Ops:
  6.5 2.3 copy-start
  6.5 627.3 %all-gather.3.cloned.1.call-start = ((), (), s32[]{:S(2)}) async-start(), calls=%async_computation.2 | async-start | bytes 135266304 | tf_op jit(solution)/shard_map/all_gather | solution.py:14
  17.9 5.4 copy-start.3
  20.2 3.2 copy-start.1
  23.4 2.4 copy-start.4
  23.4 847.0 %reduce-scatter.2.cloned.1.call-start = ((), (), s32[]{:S(2)}) async-start(), calls=%async_computation.1 | async-start | bytes 6291456 | tf_op jit(solution)/shard_map/reduce_scatter | solution.py:87
  30.8 3.8 copy-start.5
  634.3 1.8 copy-start.2
  647.3 1.8 copy-start.2
Sparse Core Ops, SparseCore 0:
  23.5 610.2 all-gather.2
  667.3 203.0 reduce-scatter.1
where the time goes:
time: 886 us; the launch traced here: 880 us
  waiting for transfers between devices  803 us (91%)
  local copies, waits for them, and re-layouts  31 us (3%)
  matrix products  25.2 us (3%)
  between operations  13.5 us (2%)
    all_gather x1, waiting for transfers between devices, carried_in(): gathered = lax.all_gather(part, axis)  599 us
    reduce_scatter x1, waiting for transfers between devices, local(): lax.psum_scatter(jnp.dot(attended, out_weight, preferred_element_type=jnp...  203 us
  transfers between devices with their start and end apart: 2, of which 2 were waited for; matrix products, arithmetic and copies ran while one was open for 1% of the time, Pallas kernels for 0%

commit v1 on v0

v1 whole, which is shorter than its diff:
```python
import jax
import jax.numpy as jnp
from jax import lax
from jax.experimental import pallas as pl
from jax.experimental.pallas import tpu as pltpu
from jax.sharding import PartitionSpec as P

MESH = pl.DeviceIdType.MESH
F32 = jnp.float32
BF16 = jnp.bfloat16
BLK = 256
NX, NY, NZ = 4, 4, 8
CHUNKS = 2
OUT_TILES = 4
EPSILON = 1e-05
ORDER = (4, 3, 5, 2, 6, 1, 7)


def dot(a, b, contract=((1,), (0,))):
    return lax.dot_general(a, b, (contract, ((), ())), preferred_element_type=F32)


def halves(squared):
    high = squared.astype(BF16)
    return high, (squared - high.astype(F32)).astype(BF16)


def kernel(
    q_hbm, k_hbm, v_hbm, f_hbm, gain_hbm, w_hbm, out_hbm,
    q_ref, k_ref, v_ref, f_ref, gain_ref, w_ref, out_ref,
    kft, qf, local, first, state_send, state_recv, y_send, y_recv, x_send, x_recv,
    prefix_send, prefix_recv, att, base,
    load_sem, out_sem, w_sems, s_ssem, s_rsem, y_ssem, y_rsem, x_ssem, x_rsem, p_ssem, p_rsem, a_ssem, a_rsem,
):
    heads, dh, m = f_ref.shape
    rows = q_ref.shape[0]
    width = heads * dh
    scale = dh ** (-0.25)
    log2e = 1.4426950408889634
    shift = 0.5 * (m.bit_length() - 1)
    part = m // CHUNKS
    me = lax.axis_index("ctx")
    core = lax.axis_index("head")
    z = lax.rem(me, NZ)
    y = lax.rem(me // NZ, NY)
    x = me // (NZ * NY)

    def at_z(d):
        return lax.rem(z + d, NZ)

    def z_device(d):
        return me - z + at_z(d)

    def y_device(d):
        return me + (lax.rem(y + d, NY) - y) * NZ

    def x_device(d):
        return me + (lax.rem(x + d, NX) - x) * (NZ * NY)

    def head_columns(h):
        return pl.ds(pl.multiple_of(h * dh, dh), dh)

    own_rows = pl.ds(pl.multiple_of(core * width, width), width)

    loads = [
        pltpu.make_async_copy(src, dst, load_sem.at[i])
        for i, (src, dst) in enumerate(
            (
                (f_hbm, f_ref),
                (k_hbm, k_ref),
                (v_hbm, v_ref),
                (q_hbm, q_ref),
                (gain_hbm, gain_ref),
                (w_hbm, w_ref.at[own_rows, :]),
            )
        )
    ]
    for load in loads:
        load.start()

    barrier = pltpu.get_barrier_semaphore()
    partners = (
        [{"ctx": z_device(d)} for d in range(1, NZ)]
        + [{"ctx": y_device(d)} for d in range(1, NY)]
        + [{"ctx": x_device(d)} for d in range(1, NX)]
        + [{"head": 1 - core}]
    )
    for partner in partners:
        pl.semaphore_signal(barrier, inc=1, device_id=partner, device_id_type=MESH)
    pl.semaphore_wait(barrier, len(partners))

    w_copy = pltpu.make_async_remote_copy(
        src_ref=w_hbm, dst_ref=w_ref.at[own_rows, :], send_sem=w_sems.at[0], recv_sem=w_sems.at[1],
        device_id={"head": 1 - core}, device_id_type=MESH,
    )
    w_copy.start()

    def state_copy(c, d):
        return pltpu.make_async_remote_copy(
            src_ref=state_send.at[c, at_z(d)], dst_ref=state_recv.at[c, z],
            send_sem=s_ssem.at[c, d], recv_sem=s_rsem.at[c, z],
            device_id={"ctx": z_device(d)}, device_id_type=MESH,
        )

    def prefix_copy(c, d):
        return pltpu.make_async_remote_copy(
            src_ref=prefix_send.at[c, at_z(d)], dst_ref=prefix_recv.at[c, z],
            send_sem=p_ssem.at[c, d], recv_sem=p_rsem.at[c, z],
            device_id={"ctx": z_device(d)}, device_id_type=MESH,
        )

    def y_copy(c, d):
        return pltpu.make_async_remote_copy(
            src_ref=y_send.at[c], dst_ref=y_recv.at[c, y], send_sem=y_ssem.at[c, d], recv_sem=y_rsem.at[c, y],
            device_id={"ctx": y_device(d)}, device_id_type=MESH,
        )

    def x_copy(c, d):
        return pltpu.make_async_remote_copy(
            src_ref=x_send.at[c], dst_ref=x_recv.at[c, x], send_sem=x_ssem.at[c, d], recv_sem=x_rsem.at[c, x],
            device_id={"ctx": x_device(d)}, device_id_type=MESH,
        )

    def arrival(ref, sem, device_id):
        return pltpu.make_async_remote_copy(
            src_ref=ref, dst_ref=ref, send_sem=sem, recv_sem=sem, device_id=device_id, device_id_type=MESH
        )

    loads[0].wait()
    loads[1].wait()
    loads[2].wait()
    ones_row = jnp.ones((8, dh), BF16)

    def key_head(h):
        cols = head_columns(h)
        k = k_ref[:, cols]
        v = v_ref[:, cols]
        linear = dot(f_ref[h].T, k, ((1,), (1,)))
        wide = k.astype(F32)
        high, low = halves(wide * wide)
        squares = (dot(ones_row, high, ((1,), (1,))) + dot(ones_row, low, ((1,), (1,))))[0:1]
        feats = jnp.exp2(
            linear * (scale * log2e) - (squares * (0.5 * scale * scale * log2e) + shift)
        ).astype(BF16)
        kft[h] = feats
        one = dot(feats[:, :BLK], v[:BLK])
        two = dot(feats[:, BLK:], v[BLK:])
        first[h] = one.astype(BF16)
        return (one + two).astype(BF16)

    def key_step(i, carry):
        d = lax.select(i % 2 == 0, NZ // 2 + i // 2, NZ // 2 - 1 - i // 2)
        d = lax.rem(d, NZ)
        h = at_z(d)
        state = key_head(h)
        for c in range(CHUNKS):
            state_send[c, h] = state[c * part : (c + 1) * part]
        state_copy(0, d).start()
        return carry

    lax.fori_loop(0, NZ - 1, key_step, 0)
    state = key_head(z)
    for c in range(CHUNKS):
        state_recv[c, z] = state[c * part : (c + 1) * part]
    for c in range(1, CHUNKS):
        for d in ORDER:
            state_copy(c, d).start()

    loads[3].wait()
    ones_square = jnp.ones((dh, dh), BF16)
    mask = lax.broadcasted_iota(jnp.int32, (BLK, BLK), 0) >= lax.broadcasted_iota(jnp.int32, (BLK, BLK), 1)

    def query_head(h, carry):
        cols = head_columns(h)
        q = q_ref[:, cols]
        wide = q.astype(F32)
        high, low = halves(wide * wide)
        squares = dot(high, ones_square) + dot(low, ones_square)
        away = squares * (0.5 * scale * scale * log2e) + shift
        linear = dot(q, f_ref[h])
        feats = jnp.exp2(
            linear * (scale * log2e) - jnp.concatenate([away] * (m // dh), axis=1)
        ).astype(BF16)
        qf[h] = feats
        for b in range(rows // BLK):
            span = slice(b * BLK, (b + 1) * BLK)
            scores = dot(feats[span], kft[h, :, span])
            weights = jnp.where(mask, scores, 0.0).astype(BF16)
            term = dot(weights, v_ref[span, cols])
            if b > 0:
                term = term + dot(feats[span], first[h])
            local[span, cols] = term
        return carry

    lax.fori_loop(0, heads, query_head, 0)

    for c in range(CHUNKS):
        for d in range(1, NZ):
            s = at_z(d)
            arrival(state_recv.at[c, s], s_rsem.at[c, s], {"ctx": z_device(d)}).wait_recv()
        total = jnp.zeros((part, dh), F32)
        for s in range(NZ):
            total = total + state_recv[c, s].astype(F32)
        line = total.astype(BF16)
        y_send[c] = line
        y_recv[c, y] = line
        for d in range(1, NY):
            y_copy(c, d).start()
        for d in range(1, NY):
            s = lax.rem(y + d, NY)
            arrival(y_recv.at[c, s], y_rsem.at[c, s], {"ctx": y_device(d)}).wait_recv()
        total = jnp.zeros((part, dh), F32)
        before = jnp.zeros((part, dh), F32)
        for s in range(NY):
            one = y_recv[c, s].astype(F32)
            total = total + one
            before = before + jnp.where(s < y, one, 0.0)
        base[...] = before
        plane = total.astype(BF16)
        x_send[c] = plane
        x_recv[c, x] = plane
        for d in range(1, NX):
            x_copy(c, d).start()
        for d in range(1, NX):
            s = lax.rem(x + d, NX)
            arrival(x_recv.at[c, s], x_rsem.at[c, s], {"ctx": x_device(d)}).wait_recv()
        running = base[...]
        for s in range(NX):
            running = running + jnp.where(s < x, x_recv[c, s].astype(F32), 0.0)
        for s in range(NZ):
            prefix_send[c, s] = running.astype(BF16)
            running = running + state_recv[c, s].astype(F32)
        prefix_recv[c, z] = prefix_send[c, z]
        for d in ORDER:
            prefix_copy(c, d).start()

    loads[4].wait()
    peer = 1 - core

    def att_copy(h):
        cols = pl.ds(pl.multiple_of(core * width + h * dh, dh), dh)
        return pltpu.make_async_remote_copy(
            src_ref=att.at[peer, :, cols], dst_ref=att.at[peer, :, cols],
            send_sem=a_ssem.at[h], recv_sem=a_rsem.at[h],
            device_id={"head": peer}, device_id_type=MESH,
        )

    def last_head(h):
        cols = head_columns(h)
        gain = gain_ref[:, cols].astype(F32)
        for b in (peer, core):
            span = pl.ds(pl.multiple_of(b * BLK, BLK), BLK)
            numerator = local[span, cols]
            for c in range(CHUNKS):
                numerator = numerator + dot(
                    qf[h, span, c * part : (c + 1) * part], prefix_recv[c, h]
                )
            mean = jnp.mean(numerator * numerator, axis=-1, keepdims=True)
            att[b, :, pl.ds(pl.multiple_of(core * width + h * dh, dh), dh)] = (
                numerator * lax.rsqrt(mean + EPSILON) * gain
            ).astype(BF16)
        att_copy(h).start()

    last_head(z)

    def last_step(i, carry):
        d = lax.select(i % 2 == 0, 1 + i // 2, NZ - 1 - i // 2)
        h = at_z(d)
        for c in range(CHUNKS):
            arrival(prefix_recv.at[c, h], p_rsem.at[c, h], {"ctx": z_device(d)}).wait_recv()
        last_head(h)
        return carry

    lax.fori_loop(0, NZ - 1, last_step, 0)

    loads[5].wait()
    w_copy.wait()
    for h in range(heads):
        cols = pl.ds(pl.multiple_of(peer * width + h * dh, dh), dh)
        arrival(att.at[core, :, cols], a_rsem.at[h], {"head": peer}).wait_recv()
    columns = w_ref.shape[1]
    tile = columns // OUT_TILES

    def out_copy(n):
        cols = pl.ds(pl.multiple_of(n * tile, tile), tile)
        return pltpu.make_async_copy(out_ref.at[:, cols], out_hbm.at[:, cols], out_sem.at[n])

    def out_step(n, carry):
        cols = pl.ds(pl.multiple_of(n * tile, tile), tile)
        out_ref[:, cols] = dot(att[core], w_ref[:, cols]).astype(BF16)
        out_copy(n).start()
        return carry

    lax.fori_loop(0, OUT_TILES, out_step, 0)

    for h in range(heads):
        att_copy(h).wait_send()
    for c in range(CHUNKS):
        for d in ORDER:
            state_copy(c, d).wait_send()
            prefix_copy(c, d).wait_send()
        for d in range(1, NY):
            y_copy(c, d).wait_send()
        for d in range(1, NX):
            x_copy(c, d).wait_send()
    for n in range(OUT_TILES):
        out_copy(n).wait()


def local(queries, key_vectors, values, features, norm_gain, out_weight):
    heads, dh, m = features.shape
    rows, width = queries.shape
    full, columns = 2 * width, out_weight.shape[1]
    part = m // CHUNKS
    dma = pltpu.SemaphoreType.DMA
    return pl.pallas_call(
        kernel,
        out_shape=jax.ShapeDtypeStruct((rows // 2, columns), BF16),
        in_specs=[pl.BlockSpec(memory_space=pl.ANY)] * 6,
        out_specs=pl.BlockSpec(memory_space=pl.ANY),
        scratch_shapes=[
            pltpu.VMEM((rows, width), BF16),
            pltpu.VMEM((rows, width), BF16),
            pltpu.VMEM((rows, width), BF16),
            pltpu.VMEM((heads, dh, m), BF16),
            pltpu.VMEM((1, width), BF16),
            pltpu.VMEM((full, columns), BF16),
            pltpu.VMEM((rows // 2, columns), BF16),
            pltpu.VMEM((heads, m, rows), BF16),
            pltpu.VMEM((heads, rows, m), BF16),
            pltpu.VMEM((rows, width), F32),
            pltpu.VMEM((heads, m, dh), BF16),
            pltpu.VMEM((CHUNKS, NZ, part, dh), BF16),
            pltpu.VMEM((CHUNKS, NZ, part, dh), BF16),
            pltpu.VMEM((CHUNKS, part, dh), BF16),
            pltpu.VMEM((CHUNKS, NY, part, dh), BF16),
            pltpu.VMEM((CHUNKS, part, dh), BF16),
            pltpu.VMEM((CHUNKS, NX, part, dh), BF16),
            pltpu.VMEM((CHUNKS, NZ, part, dh), BF16),
            pltpu.VMEM((CHUNKS, NZ, part, dh), BF16),
            pltpu.VMEM((2, rows // 2, full), BF16),
            pltpu.VMEM((part, dh), F32),
            dma((6,)),
            dma((OUT_TILES,)),
            dma((2,)),
            dma((CHUNKS, NZ)),
            dma((CHUNKS, NZ)),
            dma((CHUNKS, NY)),
            dma((CHUNKS, NY)),
            dma((CHUNKS, NX)),
            dma((CHUNKS, NX)),
            dma((CHUNKS, NZ)),
            dma((CHUNKS, NZ)),
            dma((heads,)),
            dma((heads,)),
        ],
        compiler_params=pltpu.CompilerParams(
            collective_id=0, has_side_effects=True, vmem_limit_bytes=60 * 1024 * 1024
        ),
        cost_estimate=pl.CostEstimate(flops=4 * 10**9, bytes_accessed=10**7, transcendentals=2 * 10**6),
    )(queries, key_vectors, values, features, norm_gain.reshape(1, width), out_weight)


def solution(mesh):
    return jax.shard_map(
        local,
        mesh=mesh,
        in_specs=(
            P("ctx", "head"),
            P("ctx", "head"),
            P("ctx", "head"),
            P("head", None, None),
            P("head"),
            P("head", None),
        ),
        out_specs=P(("ctx", "head"), None),
        check_vma=False,
    )
```

time: 886 us -> 53.7 us (0.06)
  waiting for transfers between devices: 803 us -> 0 us
  Pallas kernels: 0 us -> 50 us
  local copies, waits for them, and re-layouts: 31 us -> 3.58 us
  matrix products: 25.2 us -> 0 us
  between operations: 13.5 us -> 0.01 us
    all_gather x1 -> x0, waiting for transfers between devices: 599 us -> none  [carried_in(): gathered = lax.all_gather(part, axis)]
    reduce_scatter x1 -> x0, waiting for transfers between devices: 203 us -> none  [local(): lax.psum_scatter(jnp.dot(attended, out_weight, preferred_element_type=jnp...]
    pallas_call x0 -> x1, Pallas kernels: none -> 50 us  [local(): pl.pallas_call(kernel, out_shape=jax.ShapeDtypeStruct((rows // 2, columns...]
    dot_general x8 -> x0, matrix products: 25.2 us -> none  [the longest x2 6.88 us: advance(): jnp.einsum('hij,jhd->ihd', weights, value_tile_rows, preferred_element_ty...]
    dynamic_slice x8 -> x0, local copies, waits for them, and re-layouts: 9.95 us -> none  [local(): lax.scan(advance, earlier_sum, (query_feature_map, key_feature_map, value...]
  transfers between devices with their start and end apart: 2 -> 0, of which waited for: 2 -> 0; matrix products, arithmetic and copies ran while one was open for 1% -> 0% of each run, Pallas kernels for 0% -> 0%
where the time goes in v1:
time: 53.7 us; the launch traced here: 53.6 us
  Pallas kernels  50 us (93%)
  local copies, waits for them, and re-layouts  3.58 us (7%)
    pallas_call x1, Pallas kernels, local(): pl.pallas_call(kernel, out_shape=jax.ShapeDtypeStruct((rows // 2, columns...  50 us
    unnamed x1, local copies, waits for them, and re-layouts  2.3 us
    reshape x1, local copies, waits for them, and re-layouts, local(): norm_gain.reshape(1, width)  1.28 us

profile of v1, /device:TPU:1, one launch (start us, length us, event | category | flops | bytes accessed | tf_op | source)
XLA Modules:
  0.0 53.6 jit_solution(1472751402357860743)
XLA Ops:
  0.0 1.3 %reshape.3.gain_hbm = bf16[1,1024]{1,0:T(2,128)(2,1)} reshape(bf16[1024]{0:T(1024)(128)(2,1)} %param.10) | data formatting | bytes 4096 | tf_op jit(solution)/shard_map/reshape | solution.py:361
  1.3 50.0 %shard_map.64 = bf16[256,2048]{1,0:T(8,128)(2,1)} custom-call(bf16[512,1024]{1,0:T(8,128)(2,1)} %q_hbm.1, bf16[512,1024]{1,0:T(8,128)(2,1)} %k_hbm.1, bf16[512,1024]{1,0:T(8,128)(2,1)} %v_hbm.1, bf16[8,128,256]{2,1,0:T(8,128)(2,1)} %f_hbm.1, bf16[1,1024]{1,0:T(2,128)(2,1)} %reshape.3.gain_hbm, bf16[1024,2048]{1,0:T(8,128)(2,1)} %w_hbm.1), custom_call_target="tpu_custom_call" | custom-call | flops 4000000000 | bytes 10000000 | tf_op jit(solution)/shard_map/pallas_call | solution.py:316
  51.3 2.3 %copy.8 = bf16[256,2048]{1,0:T(8,128)(2,1)} copy(bf16[256,2048]{1,0:T(8,128)(2,1)} %shard_map.64) | data formatting | bytes 2097152

commit v2 on v1

v2 whole, which is shorter than its diff:
```python
import jax
import jax.numpy as jnp
from jax import lax
from jax.experimental import pallas as pl
from jax.experimental.pallas import tpu as pltpu
from jax.sharding import PartitionSpec as P

MESH = pl.DeviceIdType.MESH
F32 = jnp.float32
BF16 = jnp.bfloat16
BLK = 256
NX, NY, NZ = 4, 4, 8
NXY = NX * NY
CHUNKS = 4
OUT_TILES = 4
EPSILON = 1e-05
ORDER = (4, 3, 5, 2, 6, 1, 7)


def dot(a, b, contract=((1,), (0,))):
    return lax.dot_general(a, b, (contract, ((), ())), preferred_element_type=F32)


def halves(squared):
    high = squared.astype(BF16)
    return high, (squared - high.astype(F32)).astype(BF16)


def kernel(
    q_hbm, k_hbm, v_hbm, f_hbm, gain_hbm, w_hbm, out_ref,
    q_ref, k_ref, v_ref, f_ref, gain_ref, w_ref, kft, qf, local, first,
    state_send, state_recv, line_send, line_recv, prefix_send, prefix_recv, att, gains, acc,
    load_sem, w_sems, s_ssem, s_rsem, l_ssem, l_rsem, p_ssem, p_rsem, a_ssem, a_rsem,
):
    heads, dh, m = f_ref.shape
    rows = q_ref.shape[0]
    width = heads * dh
    per = heads // CHUNKS
    piece = m // NZ
    scale = dh ** (-0.25)
    log2e = 1.4426950408889634
    shift = 0.5 * (m.bit_length() - 1)
    me = lax.axis_index("ctx")
    core = lax.axis_index("head")
    peer = 1 - core
    z = lax.rem(me, NZ)
    w = me // NZ

    def at_z(d):
        return lax.rem(z + d, NZ)

    def z_device(d):
        return {"ctx": me - z + at_z(d)}

    def head_columns(h):
        return pl.ds(pl.multiple_of(h * dh, dh), dh)

    def heads_of(c):
        return pl.ds(c * per, per)

    def piece_of(s):
        return pl.ds(pl.multiple_of(s * piece, piece), piece)

    own_rows = pl.ds(pl.multiple_of(core * width, width), width)

    loads = [
        pltpu.make_async_copy(src, dst, load_sem.at[i])
        for i, (src, dst) in enumerate(
            (
                (f_hbm, f_ref),
                (k_hbm, k_ref),
                (v_hbm, v_ref),
                (q_hbm, q_ref),
                (gain_hbm, gain_ref),
                (w_hbm, w_ref.at[own_rows, :]),
            )
        )
    ]
    for load in loads:
        load.start()

    barrier = pltpu.get_barrier_semaphore()
    for d in range(1, NZ):
        pl.semaphore_signal(barrier, inc=1, device_id=z_device(d), device_id_type=MESH)
    for d in range(1, NXY):
        pl.semaphore_signal(
            barrier, inc=1, device_id={"ctx": lax.rem(w + d, NXY) * NZ + z}, device_id_type=MESH
        )
    pl.semaphore_signal(barrier, inc=1, device_id={"head": peer}, device_id_type=MESH)
    pl.semaphore_wait(barrier, NZ - 1 + NXY - 1 + 1)

    w_copy = pltpu.make_async_remote_copy(
        src_ref=w_hbm, dst_ref=w_ref.at[own_rows, :], send_sem=w_sems.at[0], recv_sem=w_sems.at[1],
        device_id={"head": peer}, device_id_type=MESH,
    )
    w_copy.start()

    def state_copy(c, d):
        return pltpu.make_async_remote_copy(
            src_ref=state_send.at[heads_of(c), piece_of(at_z(d))], dst_ref=state_recv.at[c, z],
            send_sem=s_ssem.at[c, d], recv_sem=s_rsem.at[c, z],
            device_id=z_device(d), device_id_type=MESH,
        )

    def line_copy(c, t):
        return pltpu.make_async_remote_copy(
            src_ref=line_send.at[c], dst_ref=line_recv.at[c, w],
            send_sem=l_ssem.at[c, t], recv_sem=l_rsem.at[c, w],
            device_id={"ctx": t * NZ + z}, device_id_type=MESH,
        )

    def prefix_copy(c, d):
        return pltpu.make_async_remote_copy(
            src_ref=prefix_send.at[c, at_z(d)], dst_ref=prefix_recv.at[heads_of(c), piece_of(z)],
            send_sem=p_ssem.at[c, d], recv_sem=p_rsem.at[c, z],
            device_id=z_device(d), device_id_type=MESH,
        )

    def att_columns(owner, c):
        return pl.ds(pl.multiple_of(owner * width + c * (per * dh), per * dh), per * dh)

    def att_copy(c):
        cols = att_columns(core, c)
        return pltpu.make_async_remote_copy(
            src_ref=att.at[peer, :, cols], dst_ref=att.at[peer, :, cols],
            send_sem=a_ssem.at[c], recv_sem=a_rsem.at[c],
            device_id={"head": peer}, device_id_type=MESH,
        )

    def arrival(ref, sem, device_id):
        return pltpu.make_async_remote_copy(
            src_ref=ref, dst_ref=ref, send_sem=sem, recv_sem=sem, device_id=device_id, device_id_type=MESH
        )

    loads[0].wait()
    loads[1].wait()
    loads[2].wait()
    ones_row = jnp.ones((8, dh), BF16)

    def key_head(h):
        cols = head_columns(h)
        k = k_ref[:, cols]
        v = v_ref[:, cols]
        linear = dot(f_ref[h].T, k, ((1,), (1,)))
        wide = k.astype(F32)
        high, low = halves(wide * wide)
        squares = (dot(ones_row, high, ((1,), (1,))) + dot(ones_row, low, ((1,), (1,))))[0:1]
        feats = jnp.exp2(
            linear * (scale * log2e) - (squares * (0.5 * scale * scale * log2e) + shift)
        ).astype(BF16)
        kft[h] = feats
        one = dot(feats[:, :BLK], v[:BLK])
        two = dot(feats[:, BLK:], v[BLK:])
        first[h] = one.astype(BF16)
        state_send[h] = (one + two).astype(BF16)

    def key_chunk(c, carry):
        for i in range(per):
            key_head(c * per + i)
        for d in ORDER:
            state_copy(c, d).start()
        state_recv[c, z] = state_send[heads_of(c), piece_of(z)]
        return carry

    lax.fori_loop(0, CHUNKS, key_chunk, 0)

    loads[3].wait()
    ones_square = jnp.ones((dh, dh), BF16)
    mask = lax.broadcasted_iota(jnp.int32, (BLK, BLK), 0) >= lax.broadcasted_iota(jnp.int32, (BLK, BLK), 1)

    def query_head(h, carry):
        cols = head_columns(h)
        q = q_ref[:, cols]
        wide = q.astype(F32)
        high, low = halves(wide * wide)
        squares = dot(high, ones_square) + dot(low, ones_square)
        away = squares * (0.5 * scale * scale * log2e) + shift
        linear = dot(q, f_ref[h])
        feats = jnp.exp2(
            linear * (scale * log2e) - jnp.concatenate([away] * (m // dh), axis=1)
        ).astype(BF16)
        qf[h] = feats
        for b in range(rows // BLK):
            span = slice(b * BLK, (b + 1) * BLK)
            scores = dot(feats[span], kft[h, :, span])
            weights = jnp.where(mask, scores, 0.0).astype(BF16)
            term = dot(weights, v_ref[span, cols])
            if b > 0:
                term = term + dot(feats[span], first[h])
            local[span, cols] = term
        return carry

    def query_chunk(c):
        lax.fori_loop(c * per, (c + 1) * per, query_head, 0)

    def line_sum(c):
        for d in range(1, NZ):
            s = at_z(d)
            arrival(state_recv.at[c, s], s_rsem.at[c, s], z_device(d)).wait_recv()
        total = jnp.zeros((per, piece, dh), F32)
        for s in range(NZ):
            total = total + state_recv[c, s].astype(F32)
        line_send[c] = total.astype(BF16)

        def send(t, carry):
            line_copy(c, t).start()
            return carry

        lax.fori_loop(w + 1, NXY, send, 0)

    def prefixes(c):
        def one(s, running):
            arrival(line_recv.at[c, s], l_rsem.at[c, s], {"ctx": s * NZ + z}).wait_recv()
            return running + line_recv[c, s].astype(F32)

        running = lax.fori_loop(0, w, one, jnp.zeros((per, piece, dh), F32))
        for s in range(NZ):
            prefix_send[c, s] = running.astype(BF16)
            running = running + state_recv[c, s].astype(F32)
        for d in ORDER:
            prefix_copy(c, d).start()
        prefix_recv[heads_of(c), piece_of(z)] = prefix_send[c, z]

    def last_chunk(c):
        for d in range(1, NZ):
            s = at_z(d)
            arrival(prefix_recv.at[heads_of(c), piece_of(s)], p_rsem.at[c, s], z_device(d)).wait_recv()
        for b in (peer, core):
            span = pl.ds(pl.multiple_of(b * BLK, BLK), BLK)
            for i in range(per):
                h = c * per + i
                numerator = local[span, head_columns(h)] + dot(qf[h, span], prefix_recv[h])
                mean = jnp.mean(numerator * numerator, axis=-1, keepdims=True)
                att[b, :, pl.ds(pl.multiple_of(core * width + h * dh, dh), dh)] = (
                    numerator * lax.rsqrt(mean + EPSILON) * gains[h : h + 1, :]
                ).astype(BF16)
            if b is peer:
                att_copy(c).start()

    def att_wait(c):
        cols = att_columns(peer, c)
        arrival(att.at[core, :, cols], a_rsem.at[c], {"head": peer}).wait_recv()

    tile = w_ref.shape[1] // OUT_TILES

    def project(blocks, start, end):
        def one(n, carry):
            cols = pl.ds(pl.multiple_of(n * tile, tile), tile)
            total = None if start else acc[:, cols]
            for block in blocks:
                product = dot(att[core, :, block], w_ref[block, cols])
                total = product if total is None else total + product
            if end:
                out_ref[:, cols] = total.astype(BF16)
            else:
                acc[:, cols] = total
            return carry

        lax.fori_loop(0, OUT_TILES, one, 0)

    query_chunk(0)
    query_chunk(1)
    line_sum(0)
    query_chunk(2)
    line_sum(1)
    query_chunk(3)
    loads[4].wait()
    wide_gain = gain_ref[...].astype(F32)
    for h in range(heads):
        gains[h : h + 1, :] = wide_gain[h * dh : (h + 1) * dh].reshape(1, dh)
    line_sum(2)
    prefixes(0)
    line_sum(3)
    prefixes(1)
    prefixes(2)
    prefixes(3)
    loads[5].wait()
    w_copy.wait()
    for c in range(CHUNKS):
        last_chunk(c)
        if c == 0:
            project([att_columns(core, c)], True, False)
        else:
            att_wait(c - 1)
            project([att_columns(core, c), att_columns(peer, c - 1)], False, False)
    att_wait(CHUNKS - 1)
    project([att_columns(peer, CHUNKS - 1)], False, True)

    for c in range(CHUNKS):
        att_copy(c).wait_send()
        for d in ORDER:
            state_copy(c, d).wait_send()
            prefix_copy(c, d).wait_send()

        def sent(t, carry):
            line_copy(c, t).wait_send()
            return carry

        lax.fori_loop(w + 1, NXY, sent, 0)


def attention(queries, key_vectors, values, features, norm_gain, out_weight):
    heads, dh, m = features.shape
    rows, width = queries.shape
    full, columns = 2 * width, out_weight.shape[1]
    slab = (heads // CHUNKS, m // NZ, dh)
    dma = pltpu.SemaphoreType.DMA
    return pl.pallas_call(
        kernel,
        out_shape=pltpu.VMEM((rows // 2, columns), BF16),
        in_specs=[pl.BlockSpec(memory_space=pl.ANY)] * 6,
        out_specs=pl.BlockSpec(memory_space=pltpu.VMEM),
        scratch_shapes=[
            pltpu.VMEM((rows, width), BF16),
            pltpu.VMEM((rows, width), BF16),
            pltpu.VMEM((rows, width), BF16),
            pltpu.VMEM((heads, dh, m), BF16),
            pltpu.VMEM((width,), BF16),
            pltpu.VMEM((full, columns), BF16),
            pltpu.VMEM((heads, m, rows), BF16),
            pltpu.VMEM((heads, rows, m), BF16),
            pltpu.VMEM((rows, width), F32),
            pltpu.VMEM((heads, m, dh), BF16),
            pltpu.VMEM((heads, m, dh), BF16),
            pltpu.VMEM((CHUNKS, NZ) + slab, BF16),
            pltpu.VMEM((CHUNKS,) + slab, BF16),
            pltpu.VMEM((CHUNKS, NXY) + slab, BF16),
            pltpu.VMEM((CHUNKS, NZ) + slab, BF16),
            pltpu.VMEM((heads, m, dh), BF16),
            pltpu.VMEM((2, rows // 2, full), BF16),
            pltpu.VMEM((heads, dh), F32),
            pltpu.VMEM((rows // 2, columns), F32),
            dma((6,)),
            dma((2,)),
            dma((CHUNKS, NZ)),
            dma((CHUNKS, NZ)),
            dma((CHUNKS, NXY)),
            dma((CHUNKS, NXY)),
            dma((CHUNKS, NZ)),
            dma((CHUNKS, NZ)),
            dma((CHUNKS,)),
            dma((CHUNKS,)),
        ],
        compiler_params=pltpu.CompilerParams(
            collective_id=0, has_side_effects=True, vmem_limit_bytes=60 * 1024 * 1024
        ),
        cost_estimate=pl.CostEstimate(flops=4 * 10**9, bytes_accessed=10**7, transcendentals=2 * 10**6),
    )(queries, key_vectors, values, features, norm_gain, out_weight)


def solution(mesh):
    return jax.shard_map(
        attention,
        mesh=mesh,
        in_specs=(
            P("ctx", "head"),
            P("ctx", "head"),
            P("ctx", "head"),
            P("head", None, None),
            P("head"),
            P("head", None),
        ),
        out_specs=P(("ctx", "head"), None),
        check_vma=False,
    )
```

time: 53.7 us -> 43.6 us (0.81)
  Pallas kernels: 50 us -> 42.6 us
  local copies, waits for them, and re-layouts: 3.58 us -> 0.97 us
    pallas_call x1, Pallas kernels: 50 us -> 42.6 us  [attention(): pl.pallas_call(kernel, out_shape=pltpu.VMEM((rows // 2, columns), BF16),...]
    unnamed x1, local copies, waits for them, and re-layouts: 2.3 us -> 0.97 us
    reshape x1 -> x0, local copies, waits for them, and re-layouts: 1.28 us -> none  [local(): norm_gain.reshape(1, width)]
where the time goes in v2:
time: 43.6 us
  Pallas kernels  42.6 us (98%)
  local copies, waits for them, and re-layouts  0.97 us (2%)
    pallas_call x1, Pallas kernels, attention(): pl.pallas_call(kernel, out_shape=pltpu.VMEM((rows // 2, columns), BF16),...  42.6 us
    unnamed x1, local copies, waits for them, and re-layouts  0.97 us

profile of v2, /device:TPU:1, one launch (start us, length us, event | category | flops | bytes accessed | tf_op | source)
XLA Modules:
  0.0 43.6 jit_solution(2936764982189698974)
XLA Ops:
  0.0 42.6 %shard_map.64 = bf16[256,2048]{1,0:T(8,128)(2,1)S(1)} custom-call(bf16[512,1024]{1,0:T(8,128)(2,1)} %q_hbm.1, bf16[512,1024]{1,0:T(8,128)(2,1)} %k_hbm.1, bf16[512,1024]{1,0:T(8,128)(2,1)} %v_hbm.1, bf16[8,128,256]{2,1,0:T(8,128)(2,1)} %f_hbm.1, bf16[1024]{0:T(1024)(128)(2,1)} %gain_hbm.1, bf16[1024,2048]{1,0:T(8,128)(2,1)} %w_hbm.1), custom_call_target="tpu_custom_call" | custom-call | flops 4000000000 | bytes 10000000 | tf_op jit(solution)/shard_map/pallas_call | solution.py:308
  42.6 1.0 %copy.8 = bf16[256,2048]{1,0:T(8,128)(2,1)} copy(bf16[256,2048]{1,0:T(8,128)(2,1)S(1)} %shard_map.64) | data formatting | bytes 2097152

commit v3 on v2

--- a/solution.py
+++ b/solution.py
@@ -11,7 +11,19 @@
 BLK = 256
 NX, NY, NZ = 4, 4, 8
 NXY = NX * NY
-CHUNKS = 4
+SIZES = (2, 2, 2, 2)
+CHUNKS = len(SIZES)
+STARTS = tuple(sum(SIZES[:c]) for c in range(CHUNKS))
+SCHEDULE = (
+    ("line", 0, 2),
+    ("line", 1, 1),
+    ("line", 2, 1),
+    ("prefix", 0, 0),
+    ("line", 3, 0),
+    ("prefix", 1, 0),
+    ("prefix", 2, 0),
+    ("prefix", 3, 0),
+)
 OUT_TILES = 4
 EPSILON = 1e-05
 ORDER = (4, 3, 5, 2, 6, 1, 7)
@@ -30,12 +42,11 @@
     q_hbm, k_hbm, v_hbm, f_hbm, gain_hbm, w_hbm, out_ref,
     q_ref, k_ref, v_ref, f_ref, gain_ref, w_ref, kft, qf, local, first,
     state_send, state_recv, line_send, line_recv, prefix_send, prefix_recv, att, gains, acc,
-    load_sem, w_sems, s_ssem, s_rsem, l_ssem, l_rsem, p_ssem, p_rsem, a_ssem, a_rsem,
+    load_sem, kv_sems, w_sems, s_ssem, s_rsem, l_ssem, l_rsem, p_ssem, p_rsem, a_ssem, a_rsem,
 ):
     heads, dh, m = f_ref.shape
     rows = q_ref.shape[0]
     width = heads * dh
-    per = heads // CHUNKS
     piece = m // NZ
     scale = dh ** (-0.25)
     log2e = 1.4426950408889634
@@ -56,28 +67,28 @@
         return pl.ds(pl.multiple_of(h * dh, dh), dh)
 
     def heads_of(c):
-        return pl.ds(c * per, per)
+        return pl.ds(STARTS[c], SIZES[c])
 
     def piece_of(s):
         return pl.ds(pl.multiple_of(s * piece, piece), piece)
 
     own_rows = pl.ds(pl.multiple_of(core * width, width), width)
+
+    def chunk_load(i, c):
+        src, dst = ((k_hbm, k_ref), (v_hbm, v_ref))[i]
+        cols = pl.ds(STARTS[c] * dh, SIZES[c] * dh)
+        return pltpu.make_async_copy(src.at[:, cols], dst.at[:, cols], kv_sems.at[i, c])
 
     loads = [
         pltpu.make_async_copy(src, dst, load_sem.at[i])
         for i, (src, dst) in enumerate(
-            (
-                (f_hbm, f_ref),
-                (k_hbm, k_ref),
-                (v_hbm, v_ref),
-                (q_hbm, q_ref),
-                (gain_hbm, gain_ref),
-                (w_hbm, w_ref.at[own_rows, :]),
-            )
+            ((f_hbm, f_ref), (q_hbm, q_ref), (gain_hbm, gain_ref), (w_hbm, w_ref.at[own_rows, :]))
         )
     ]
-    for load in loads:
-        load.start()
+    loads[0].start()
+    for c in range(CHUNKS):
+        chunk_load(0, c).start()
+        chunk_load(1, c).start()
 
     barrier = pltpu.get_barrier_semaphore()
     for d in range(1, NZ):
@@ -87,37 +98,35 @@
             barrier, inc=1, device_id={"ctx": lax.rem(w + d, NXY) * NZ + z}, device_id_type=MESH
         )
     pl.semaphore_signal(barrier, inc=1, device_id={"head": peer}, device_id_type=MESH)
-    pl.semaphore_wait(barrier, NZ - 1 + NXY - 1 + 1)
 
     w_copy = pltpu.make_async_remote_copy(
         src_ref=w_hbm, dst_ref=w_ref.at[own_rows, :], send_sem=w_sems.at[0], recv_sem=w_sems.at[1],
         device_id={"head": peer}, device_id_type=MESH,
     )
-    w_copy.start()
 
     def state_copy(c, d):
         return pltpu.make_async_remote_copy(
-            src_ref=state_send.at[heads_of(c), piece_of(at_z(d))], dst_ref=state_recv.at[c, z],
+            src_ref=state_send.at[heads_of(c), piece_of(at_z(d))], dst_ref=state_recv.at[z, heads_of(c)],
             send_sem=s_ssem.at[c, d], recv_sem=s_rsem.at[c, z],
             device_id=z_device(d), device_id_type=MESH,
         )
 
     def line_copy(c, t):
         return pltpu.make_async_remote_copy(
-            src_ref=line_send.at[c], dst_ref=line_recv.at[c, w],
+            src_ref=line_send.at[heads_of(c)], dst_ref=line_recv.at[w, heads_of(c)],
             send_sem=l_ssem.at[c, t], recv_sem=l_rsem.at[c, w],
             device_id={"ctx": t * NZ + z}, device_id_type=MESH,
         )
 
     def prefix_copy(c, d):
         return pltpu.make_async_remote_copy(
-            src_ref=prefix_send.at[c, at_z(d)], dst_ref=prefix_recv.at[heads_of(c), piece_of(z)],
+            src_ref=prefix_send.at[at_z(d), heads_of(c)], dst_ref=prefix_recv.at[heads_of(c), piece_of(z)],
             send_sem=p_ssem.at[c, d], recv_sem=p_rsem.at[c, z],
             device_id=z_device(d), device_id_type=MESH,
         )
 
     def att_columns(owner, c):
-        return pl.ds(pl.multiple_of(owner * width + c * (per * dh), per * dh), per * dh)
+        return pl.ds(pl.multiple_of(owner * width + STARTS[c] * dh, dh), SIZES[c] * dh)
 
     def att_copy(c):
         cols = att_columns(core, c)
@@ -133,8 +142,6 @@
         )
 
     loads[0].wait()
-    loads[1].wait()
-    loads[2].wait()
     ones_row = jnp.ones((8, dh), BF16)
 
     def key_head(h):
@@ -154,17 +161,22 @@
         first[h] = one.astype(BF16)
         state_send[h] = (one + two).astype(BF16)
 
-    def key_chunk(c, carry):
-        for i in range(per):
-            key_head(c * per + i)
+    for c in range(CHUNKS):
+        chunk_load(0, c).wait()
+        chunk_load(1, c).wait()
+        for i in range(SIZES[c]):
+            key_head(STARTS[c] + i)
+        if c == 0:
+            pl.semaphore_wait(barrier, NZ - 1 + NXY - 1 + 1)
         for d in ORDER:
             state_copy(c, d).start()
-        state_recv[c, z] = state_send[heads_of(c), piece_of(z)]
-        return carry
-
-    lax.fori_loop(0, CHUNKS, key_chunk, 0)
-
-    loads[3].wait()
+        state_recv[z, heads_of(c)] = state_send[heads_of(c), piece_of(z)]
+        if c == 0:
+            for load in loads[1:]:
+                load.start()
+            w_copy.start()
+
+    loads[1].wait()
     ones_square = jnp.ones((dh, dh), BF16)
     mask = lax.broadcasted_iota(jnp.int32, (BLK, BLK), 0) >= lax.broadcasted_iota(jnp.int32, (BLK, BLK), 1)
 
@@ -191,16 +203,16 @@
         return carry
 
     def query_chunk(c):
-        lax.fori_loop(c * per, (c + 1) * per, query_head, 0)
+        lax.fori_loop(STARTS[c], STARTS[c] + SIZES[c], query_head, 0)
 
     def line_sum(c):
         for d in range(1, NZ):
             s = at_z(d)
-            arrival(state_recv.at[c, s], s_rsem.at[c, s], z_device(d)).wait_recv()
-        total = jnp.zeros((per, piece, dh), F32)
+            arrival(state_recv.at[s, heads_of(c)], s_rsem.at[c, s], z_device(d)).wait_recv()
+        total = jnp.zeros((SIZES[c], piece, dh), F32)
         for s in range(NZ):
-            total = total + state_recv[c, s].astype(F32)
-        line_send[c] = total.astype(BF16)
+            total = total + state_recv[s, heads_of(c)].astype(F32)
+        line_send[heads_of(c)] = total.astype(BF16)
 
         def send(t, carry):
             line_copy(c, t).start()
@@ -210,16 +222,16 @@
 
     def prefixes(c):
         def one(s, running):
-            arrival(line_recv.at[c, s], l_rsem.at[c, s], {"ctx": s * NZ + z}).wait_recv()
-            return running + line_recv[c, s].astype(F32)
-
-        running = lax.fori_loop(0, w, one, jnp.zeros((per, piece, dh), F32))
+            arrival(line_recv.at[s, heads_of(c)], l_rsem.at[c, s], {"ctx": s * NZ + z}).wait_recv()
+            return running + line_recv[s, heads_of(c)].astype(F32)
+
+        running = lax.fori_loop(0, w, one, jnp.zeros((SIZES[c], piece, dh), F32))
         for s in range(NZ):
-            prefix_send[c, s] = running.astype(BF16)
-            running = running + state_recv[c, s].astype(F32)
+            prefix_send[s, heads_of(c)] = running.astype(BF16)
+            running = running + state_recv[s, heads_of(c)].astype(F32)
         for d in ORDER:
             prefix_copy(c, d).start()
-        prefix_recv[heads_of(c), piece_of(z)] = prefix_send[c, z]
+        prefix_recv[heads_of(c), piece_of(z)] = prefix_send[z, heads_of(c)]
 
     def last_chunk(c):
         for d in range(1, NZ):
@@ -227,8 +239,8 @@
             arrival(prefix_recv.at[heads_of(c), piece_of(s)], p_rsem.at[c, s], z_device(d)).wait_recv()
         for b in (peer, core):
             span = pl.ds(pl.multiple_of(b * BLK, BLK), BLK)
-            for i in range(per):
-                h = c * per + i
+            for i in range(SIZES[c]):
+                h = STARTS[c] + i
                 numerator = local[span, head_columns(h)] + dot(qf[h, span], prefix_recv[h])
                 mean = jnp.mean(numerator * numerator, axis=-1, keepdims=True)
                 att[b, :, pl.ds(pl.multiple_of(core * width + h * dh, dh), dh)] = (
@@ -258,52 +270,54 @@
 
         lax.fori_loop(0, OUT_TILES, one, 0)
 
-    query_chunk(0)
-    query_chunk(1)
-    line_sum(0)
-    query_chunk(2)
-    line_sum(1)
-    query_chunk(3)
-    loads[4].wait()
+    waiting = list(range(CHUNKS))
+    for name, c, queries in SCHEDULE:
+        for _ in range(queries):
+            query_chunk(waiting.pop(0))
+        if name == "line":
+            line_sum(c)
+        else:
+            prefixes(c)
+    loads[2].wait()
     wide_gain = gain_ref[...].astype(F32)
     for h in range(heads):
         gains[h : h + 1, :] = wide_gain[h * dh : (h + 1) * dh].reshape(1, dh)
-    line_sum(2)
-    prefixes(0)
-    line_sum(3)
-    prefixes(1)
-    prefixes(2)
-    prefixes(3)
-    loads[5].wait()
+    loads[3].wait()
     w_copy.wait()
+
+    for c in range(CHUNKS):
+        for d in ORDER:
+            state_copy(c, d).wait_send()
+
+        def sent(t, carry):
+            line_copy(c, t).wait_send()
+            return carry
+
+        lax.fori_loop(w + 1, NXY, sent, 0)
+
     for c in range(CHUNKS):
         last_chunk(c)
+        if c > 0:
+            att_copy(c - 1).wait_send()
         if c == 0:
             project([att_columns(core, c)], True, False)
         else:
             att_wait(c - 1)
             project([att_columns(core, c), att_columns(peer, c - 1)], False, False)
+    for c in range(CHUNKS):
+        for d in ORDER:
+            prefix_copy(c, d).wait_send()
     att_wait(CHUNKS - 1)
     project([att_columns(peer, CHUNKS - 1)], False, True)
 
-    for c in range(CHUNKS):
-        att_copy(c).wait_send()
-        for d in ORDER:
-            state_copy(c, d).wait_send()
-            prefix_copy(c, d).wait_send()
-
-        def sent(t, carry):
-            line_copy(c, t).wait_send()
-            return carry
-
-        lax.fori_loop(w + 1, NXY, sent, 0)
+    att_copy(CHUNKS - 1).wait_send()
 
 
 def attention(queries, key_vectors, values, features, norm_gain, out_weight):
     heads, dh, m = features.shape
     rows, width = queries.shape
     full, columns = 2 * width, out_weight.shape[1]
-    slab = (heads // CHUNKS, m // NZ, dh)
+    slab = (heads, m // NZ, dh)
     dma = pltpu.SemaphoreType.DMA
     return pl.pallas_call(
         kernel,
@@ -322,15 +336,16 @@
             pltpu.VMEM((rows, width), F32),
             pltpu.VMEM((heads, m, dh), BF16),
             pltpu.VMEM((heads, m, dh), BF16),
-            pltpu.VMEM((CHUNKS, NZ) + slab, BF16),
-            pltpu.VMEM((CHUNKS,) + slab, BF16),
-            pltpu.VMEM((CHUNKS, NXY) + slab, BF16),
-            pltpu.VMEM((CHUNKS, NZ) + slab, BF16),
+            pltpu.VMEM((NZ,) + slab, BF16),
+            pltpu.VMEM(slab, BF16),
+            pltpu.VMEM((NXY,) + slab, BF16),
+            pltpu.VMEM((NZ,) + slab, BF16),
             pltpu.VMEM((heads, m, dh), BF16),
             pltpu.VMEM((2, rows // 2, full), BF16),
             pltpu.VMEM((heads, dh), F32),
             pltpu.VMEM((rows // 2, columns), F32),
-            dma((6,)),
+            dma((4,)),
+            dma((2, CHUNKS)),
             dma((2,)),
             dma((CHUNKS, NZ)),
             dma((CHUNKS, NZ)),

time: 43.6 us -> 42.5 us (0.975)
  Pallas kernels: 42.6 us -> 41.4 us
    pallas_call x1, Pallas kernels: 42.6 us -> 41.4 us  [attention(): pl.pallas_call(kernel, out_shape=pltpu.VMEM((rows // 2, columns), BF16),...]
where the time goes in v3:
time: 42.5 us; the launch traced here: 42.4 us
  Pallas kernels  41.4 us (97%)
  local copies, waits for them, and re-layouts  0.97 us (2%)
    pallas_call x1, Pallas kernels, attention(): pl.pallas_call(kernel, out_shape=pltpu.VMEM((rows // 2, columns), BF16),...  41.4 us
    unnamed x1, local copies, waits for them, and re-layouts  0.97 us

profile of v3, /device:TPU:1, one launch (start us, length us, event | category | flops | bytes accessed | tf_op | source)
XLA Modules:
  0.0 42.4 jit_solution(5936780144049211972)
XLA Ops:
  0.0 41.4 %shard_map.64 = bf16[256,2048]{1,0:T(8,128)(2,1)S(1)} custom-call(bf16[512,1024]{1,0:T(8,128)(2,1)} %q_hbm.1, bf16[512,1024]{1,0:T(8,128)(2,1)} %k_hbm.1, bf16[512,1024]{1,0:T(8,128)(2,1)} %v_hbm.1, bf16[8,128,256]{2,1,0:T(8,128)(2,1)} %f_hbm.1, bf16[1024]{0:T(1024)(128)(2,1)} %gain_hbm.1, bf16[1024,2048]{1,0:T(8,128)(2,1)} %w_hbm.1), custom_call_target="tpu_custom_call" | custom-call | flops 4000000000 | bytes 10000000 | tf_op jit(solution)/shard_map/pallas_call | solution.py:322
  41.4 1.0 %copy.8 = bf16[256,2048]{1,0:T(8,128)(2,1)} copy(bf16[256,2048]{1,0:T(8,128)(2,1)S(1)} %shard_map.64) | data formatting | bytes 2097152

commit v4 on v3

--- a/solution.py
+++ b/solution.py
@@ -107,7 +107,7 @@
     def state_copy(c, d):
         return pltpu.make_async_remote_copy(
             src_ref=state_send.at[heads_of(c), piece_of(at_z(d))], dst_ref=state_recv.at[z, heads_of(c)],
-            send_sem=s_ssem.at[c, d], recv_sem=s_rsem.at[c, z],
+            send_sem=s_ssem.at[c], recv_sem=s_rsem.at[c],
             device_id=z_device(d), device_id_type=MESH,
         )
 
@@ -121,7 +121,7 @@
     def prefix_copy(c, d):
         return pltpu.make_async_remote_copy(
             src_ref=prefix_send.at[at_z(d), heads_of(c)], dst_ref=prefix_recv.at[heads_of(c), piece_of(z)],
-            send_sem=p_ssem.at[c, d], recv_sem=p_rsem.at[c, z],
+            send_sem=p_ssem.at[c], recv_sem=p_rsem.at[c],
             device_id=z_device(d), device_id_type=MESH,
         )
 
@@ -139,6 +139,13 @@
     def arrival(ref, sem, device_id):
         return pltpu.make_async_remote_copy(
             src_ref=ref, dst_ref=ref, send_sem=sem, recv_sem=sem, device_id=device_id, device_id_type=MESH
+        )
+
+    def all_pieces(c, send_sem, recv_sem):
+        ref = prefix_recv.at[heads_of(c), pl.ds(0, (NZ - 1) * piece)]
+        return pltpu.make_async_remote_copy(
+            src_ref=ref, dst_ref=ref, send_sem=send_sem.at[c], recv_sem=recv_sem.at[c],
+            device_id=z_device(1), device_id_type=MESH,
         )
 
     loads[0].wait()
@@ -206,9 +213,7 @@
         lax.fori_loop(STARTS[c], STARTS[c] + SIZES[c], query_head, 0)
 
     def line_sum(c):
-        for d in range(1, NZ):
-            s = at_z(d)
-            arrival(state_recv.at[s, heads_of(c)], s_rsem.at[c, s], z_device(d)).wait_recv()
+        all_pieces(c, s_ssem, s_rsem).wait_recv()
         total = jnp.zeros((SIZES[c], piece, dh), F32)
         for s in range(NZ):
             total = total + state_recv[s, heads_of(c)].astype(F32)
@@ -234,9 +239,7 @@
         prefix_recv[heads_of(c), piece_of(z)] = prefix_send[z, heads_of(c)]
 
     def last_chunk(c):
-        for d in range(1, NZ):
-            s = at_z(d)
-            arrival(prefix_recv.at[heads_of(c), piece_of(s)], p_rsem.at[c, s], z_device(d)).wait_recv()
+        all_pieces(c, p_ssem, p_rsem).wait_recv()
         for b in (peer, core):
             span = pl.ds(pl.multiple_of(b * BLK, BLK), BLK)
             for i in range(SIZES[c]):
@@ -286,8 +289,7 @@
     w_copy.wait()
 
     for c in range(CHUNKS):
-        for d in ORDER:
-            state_copy(c, d).wait_send()
+        all_pieces(c, s_ssem, s_rsem).wait_send()
 
         def sent(t, carry):
             line_copy(c, t).wait_send()
@@ -305,8 +307,7 @@
             att_wait(c - 1)
             project([att_columns(core, c), att_columns(peer, c - 1)], False, False)
     for c in range(CHUNKS):
-        for d in ORDER:
-            prefix_copy(c, d).wait_send()
+        all_pieces(c, p_ssem, p_rsem).wait_send()
     att_wait(CHUNKS - 1)
     project([att_columns(peer, CHUNKS - 1)], False, True)
 
@@ -347,12 +348,12 @@
             dma((4,)),
             dma((2, CHUNKS)),
             dma((2,)),
-            dma((CHUNKS, NZ)),
-            dma((CHUNKS, NZ)),
+            dma((CHUNKS,)),
+            dma((CHUNKS,)),
             dma((CHUNKS, NXY)),
             dma((CHUNKS, NXY)),
-            dma((CHUNKS, NZ)),
-            dma((CHUNKS, NZ)),
+            dma((CHUNKS,)),
+            dma((CHUNKS,)),
             dma((CHUNKS,)),
             dma((CHUNKS,)),
         ],

time: 42.5 us -> 41.4 us (0.974)
  Pallas kernels: 41.4 us -> 40.3 us
    pallas_call x1, Pallas kernels: 41.4 us -> 40.3 us  [attention(): pl.pallas_call(kernel, out_shape=pltpu.VMEM((rows // 2, columns), BF16),...]
where the time goes in v4:
time: 41.4 us; the launch traced here: 41.3 us
  Pallas kernels  40.3 us (97%)
  local copies, waits for them, and re-layouts  0.97 us (2%)
    pallas_call x1, Pallas kernels, attention(): pl.pallas_call(kernel, out_shape=pltpu.VMEM((rows // 2, columns), BF16),...  40.3 us
    unnamed x1, local copies, waits for them, and re-layouts  0.97 us

profile of v4, /device:TPU:1, one launch (start us, length us, event | category | flops | bytes accessed | tf_op | source)
XLA Modules:
  0.0 41.3 jit_solution(12354039291788281781)
XLA Ops:
  0.0 40.3 %shard_map.64 = bf16[256,2048]{1,0:T(8,128)(2,1)S(1)} custom-call(bf16[512,1024]{1,0:T(8,128)(2,1)} %q_hbm.1, bf16[512,1024]{1,0:T(8,128)(2,1)} %k_hbm.1, bf16[512,1024]{1,0:T(8,128)(2,1)} %v_hbm.1, bf16[8,128,256]{2,1,0:T(8,128)(2,1)} %f_hbm.1, bf16[1024]{0:T(1024)(128)(2,1)} %gain_hbm.1, bf16[1024,2048]{1,0:T(8,128)(2,1)} %w_hbm.1), custom_call_target="tpu_custom_call" | custom-call | flops 4000000000 | bytes 10000000 | tf_op jit(solution)/shard_map/pallas_call | solution.py:323
  40.3 1.0 %copy.8 = bf16[256,2048]{1,0:T(8,128)(2,1)} copy(bf16[256,2048]{1,0:T(8,128)(2,1)S(1)} %shard_map.64) | data formatting | bytes 2097152

commit v5 on v4

--- a/solution.py
+++ b/solution.py
@@ -17,14 +17,14 @@
 SCHEDULE = (
     ("line", 0, 2),
     ("line", 1, 1),
-    ("line", 2, 1),
     ("prefix", 0, 0),
+    ("line", 2, 0),
+    ("prefix", 1, 1),
     ("line", 3, 0),
-    ("prefix", 1, 0),
     ("prefix", 2, 0),
     ("prefix", 3, 0),
 )
-OUT_TILES = 4
+OUT_TILES = 1
 EPSILON = 1e-05
 ORDER = (4, 3, 5, 2, 6, 1, 7)
 
@@ -69,9 +69,6 @@
     def heads_of(c):
         return pl.ds(STARTS[c], SIZES[c])
 
-    def piece_of(s):
-        return pl.ds(pl.multiple_of(s * piece, piece), piece)
-
     own_rows = pl.ds(pl.multiple_of(core * width, width), width)
 
     def chunk_load(i, c):
@@ -86,17 +83,18 @@
         )
     ]
     loads[0].start()
-    for c in range(CHUNKS):
-        chunk_load(0, c).start()
-        chunk_load(1, c).start()
+    chunk_load(0, 0).start()
+    chunk_load(1, 0).start()
 
     barrier = pltpu.get_barrier_semaphore()
     for d in range(1, NZ):
         pl.semaphore_signal(barrier, inc=1, device_id=z_device(d), device_id_type=MESH)
-    for d in range(1, NXY):
-        pl.semaphore_signal(
-            barrier, inc=1, device_id={"ctx": lax.rem(w + d, NXY) * NZ + z}, device_id_type=MESH
-        )
+
+    def greet(t, carry):
+        pl.semaphore_signal(barrier, inc=1, device_id={"ctx": t * NZ + z}, device_id_type=MESH)
+        return carry
+
+    lax.fori_loop(0, w, greet, 0)
     pl.semaphore_signal(barrier, inc=1, device_id={"head": peer}, device_id_type=MESH)
 
     w_copy = pltpu.make_async_remote_copy(
@@ -106,7 +104,7 @@
 
     def state_copy(c, d):
         return pltpu.make_async_remote_copy(
-            src_ref=state_send.at[heads_of(c), piece_of(at_z(d))], dst_ref=state_recv.at[z, heads_of(c)],
+            src_ref=state_send.at[at_z(d), heads_of(c)], dst_ref=state_recv.at[z, heads_of(c)],
             send_sem=s_ssem.at[c], recv_sem=s_rsem.at[c],
             device_id=z_device(d), device_id_type=MESH,
         )
@@ -120,7 +118,7 @@
 
     def prefix_copy(c, d):
         return pltpu.make_async_remote_copy(
-            src_ref=prefix_send.at[at_z(d), heads_of(c)], dst_ref=prefix_recv.at[heads_of(c), piece_of(z)],
+            src_ref=prefix_send.at[at_z(d), heads_of(c)], dst_ref=prefix_recv.at[z, heads_of(c)],
             send_sem=p_ssem.at[c], recv_sem=p_rsem.at[c],
             device_id=z_device(d), device_id_type=MESH,
         )
@@ -142,7 +140,7 @@
         )
 
     def all_pieces(c, send_sem, recv_sem):
-        ref = prefix_recv.at[heads_of(c), pl.ds(0, (NZ - 1) * piece)]
+        ref = prefix_recv.at[pl.ds(0, NZ - 1), heads_of(c)]
         return pltpu.make_async_remote_copy(
             src_ref=ref, dst_ref=ref, send_sem=send_sem.at[c], recv_sem=recv_sem.at[c],
             device_id=z_device(1), device_id_type=MESH,
@@ -158,7 +156,7 @@
         linear = dot(f_ref[h].T, k, ((1,), (1,)))
         wide = k.astype(F32)
         high, low = halves(wide * wide)
-        squares = (dot(ones_row, high, ((1,), (1,))) + dot(ones_row, low, ((1,), (1,))))[0:1]
+        squares = dot(jnp.ones((8, 2 * dh), BF16), jnp.concatenate([high, low], axis=1), ((1,), (1,)))[0:1]
         feats = jnp.exp2(
             linear * (scale * log2e) - (squares * (0.5 * scale * scale * log2e) + shift)
         ).astype(BF16)
@@ -166,18 +164,22 @@
         one = dot(feats[:, :BLK], v[:BLK])
         two = dot(feats[:, BLK:], v[BLK:])
         first[h] = one.astype(BF16)
-        state_send[h] = (one + two).astype(BF16)
+        state_send[:, h] = (one + two).astype(BF16).reshape(NZ, piece, dh)
 
     for c in range(CHUNKS):
         chunk_load(0, c).wait()
         chunk_load(1, c).wait()
+        if c == 0:
+            for later in range(1, CHUNKS):
+                chunk_load(0, later).start()
+                chunk_load(1, later).start()
         for i in range(SIZES[c]):
             key_head(STARTS[c] + i)
         if c == 0:
-            pl.semaphore_wait(barrier, NZ - 1 + NXY - 1 + 1)
+            pl.semaphore_wait(barrier, NZ - 1 + NXY - 1 - w + 1)
         for d in ORDER:
             state_copy(c, d).start()
-        state_recv[z, heads_of(c)] = state_send[heads_of(c), piece_of(z)]
+        state_recv[z, heads_of(c)] = state_send[z, heads_of(c)]
         if c == 0:
             for load in loads[1:]:
                 load.start()
@@ -236,7 +238,7 @@
             running = running + state_recv[s, heads_of(c)].astype(F32)
         for d in ORDER:
             prefix_copy(c, d).start()
-        prefix_recv[heads_of(c), piece_of(z)] = prefix_send[z, heads_of(c)]
+        prefix_recv[z, heads_of(c)] = prefix_send[z, heads_of(c)]
 
     def last_chunk(c):
         all_pieces(c, p_ssem, p_rsem).wait_recv()
@@ -244,7 +246,7 @@
             span = pl.ds(pl.multiple_of(b * BLK, BLK), BLK)
             for i in range(SIZES[c]):
                 h = STARTS[c] + i
-                numerator = local[span, head_columns(h)] + dot(qf[h, span], prefix_recv[h])
+                numerator = local[span, head_columns(h)] + dot(qf[h, span], prefix_recv[:, h].reshape(m, dh))
                 mean = jnp.mean(numerator * numerator, axis=-1, keepdims=True)
                 att[b, :, pl.ds(pl.multiple_of(core * width + h * dh, dh), dh)] = (
                     numerator * lax.rsqrt(mean + EPSILON) * gains[h : h + 1, :]
@@ -271,7 +273,7 @@
                 acc[:, cols] = total
             return carry
 
-        lax.fori_loop(0, OUT_TILES, one, 0)
+        lax.fori_loop(0, OUT_TILES, one, 0, unroll=True)
 
     waiting = list(range(CHUNKS))
     for name, c, queries in SCHEDULE:
@@ -336,12 +338,12 @@
             pltpu.VMEM((heads, rows, m), BF16),
             pltpu.VMEM((rows, width), F32),
             pltpu.VMEM((heads, m, dh), BF16),
-            pltpu.VMEM((heads, m, dh), BF16),
+            pltpu.VMEM((NZ,) + slab, BF16),
             pltpu.VMEM((NZ,) + slab, BF16),
             pltpu.VMEM(slab, BF16),
             pltpu.VMEM((NXY,) + slab, BF16),
             pltpu.VMEM((NZ,) + slab, BF16),
-            pltpu.VMEM((heads, m, dh), BF16),
+            pltpu.VMEM((NZ,) + slab, BF16),
             pltpu.VMEM((2, rows // 2, full), BF16),
             pltpu.VMEM((heads, dh), F32),
             pltpu.VMEM((rows // 2, columns), F32),

time: 41.4 us -> 40.3 us (0.973)
  Pallas kernels: 40.3 us -> 39.3 us
    pallas_call x1, Pallas kernels: 40.3 us -> 39.3 us  [attention(): pl.pallas_call(kernel, out_shape=pltpu.VMEM((rows // 2, columns), BF16),...]
where the time goes in v5:
time: 40.3 us; the launch traced here: 40.2 us
  Pallas kernels  39.3 us (98%)
  local copies, waits for them, and re-layouts  0.97 us (2%)
    pallas_call x1, Pallas kernels, attention(): pl.pallas_call(kernel, out_shape=pltpu.VMEM((rows // 2, columns), BF16),...  39.3 us
    unnamed x1, local copies, waits for them, and re-layouts  0.97 us

profile of v5, /device:TPU:1, one launch (start us, length us, event | category | flops | bytes accessed | tf_op | source)
XLA Modules:
  0.0 40.2 jit_solution(2965587894750646971)
XLA Ops:
  0.0 39.3 %shard_map.64 = bf16[256,2048]{1,0:T(8,128)(2,1)S(1)} custom-call(bf16[512,1024]{1,0:T(8,128)(2,1)} %q_hbm.1, bf16[512,1024]{1,0:T(8,128)(2,1)} %k_hbm.1, bf16[512,1024]{1,0:T(8,128)(2,1)} %v_hbm.1, bf16[8,128,256]{2,1,0:T(8,128)(2,1)} %f_hbm.1, bf16[1024]{0:T(1024)(128)(2,1)} %gain_hbm.1, bf16[1024,2048]{1,0:T(8,128)(2,1)} %w_hbm.1), custom_call_target="tpu_custom_call" | custom-call | flops 4000000000 | bytes 10000000 | tf_op jit(solution)/shard_map/pallas_call | solution.py:325
  39.3 1.0 %copy.8 = bf16[256,2048]{1,0:T(8,128)(2,1)} copy(bf16[256,2048]{1,0:T(8,128)(2,1)S(1)} %shard_map.64) | data formatting | bytes 2097152
